TPU v7x, 32 devices: a whole 2x2x4 slice. The times are simulated.
32 devices in a mesh: seq: 4 (over y, x), mp: 8 (over z, core).
Axes of the slice: x: 2, y: 2, z: 4, core: 2. Of those that a mesh axis runs over, the one named last changes fastest.
Arguments:
- queries: bfloat16 [4, 8, 1280, 256], P('seq', 'mp'), may hold values from -6 to 6
- key_rows: bfloat16 [4, 8, 1280, 128], P('seq', 'mp'), may hold values from -6 to 6
- value_rows: bfloat16 [4, 8, 1280, 128], P('seq', 'mp'), may hold values from -6 to 6
Outputs:
- attended: bfloat16 [4, 8, 1280, 256], P('seq', 'mp')
All inputs are finite; a program needn't handle non-finite values.
Results may differ from a plain program's by a relative error of at most 0.0055.
Values may be sent and summed in bfloat16 or wider, within the bound.
A program may use at most 64 MiB of HBM per device.

v0:
```python
import jax
import jax.numpy as jnp
from jax import lax
from jax.sharding import PartitionSpec as P

KVH = 8
QPK = 2
WINDOW = 1024


scale_factor = 168.0 ** (-0.5)


def passed_along(block, axis, distance):
    devices = range(lax.axis_size(axis))
    route = [(i - distance, i) for i in devices if i - distance in devices]
    return lax.ppermute(block, axis, route)


def block_size(total_rows):
    size_now = total_rows
    while size_now > 1024 and size_now % 2 == 0:
        size_now = size_now // 2
    return size_now


def masked_scores(query_tile, key_tile, valid):
    raw = (
        jnp.einsum("qd,kd->qk", query_tile, key_tile, preferred_element_type=jnp.float32)
        * scale_factor
    )
    return jnp.where(valid, raw, -jnp.inf)


def joined_context(scores, value_tile):
    row_top = jnp.max(scores, axis=1, keepdims=True)
    probable = jnp.exp(scores - row_top)
    row_total = jnp.sum(probable, axis=1, keepdims=True)
    weights = probable.astype(jnp.bfloat16)
    return jnp.dot(weights, value_tile, preferred_element_type=jnp.float32) / row_total


def per_device(queries, key_rows, value_rows):
    row_count = queries.shape[2]
    head_size = key_rows.shape[3]
    model_count = lax.axis_size("mp")
    block_count = model_count // KVH
    row_block = lax.axis_index("mp") // KVH
    opening = jnp.logical_and(lax.axis_index("seq") == 0, row_block == 0)
    query_local = queries[0, 0]
    local_pair = jnp.stack([key_rows[0, 0], value_rows[0, 0]])
    if block_count > 1:
        inside = passed_along(local_pair, "mp", KVH)
        turned = passed_along(local_pair, "mp", KVH - model_count)
    else:
        inside = jnp.zeros_like(local_pair)
        turned = local_pair
    crossed = passed_along(turned, "seq", 1)
    borrowed = jnp.where(row_block == 0, crossed, inside)
    borrowed_rows = borrowed.shape[1]
    query_block = block_size(row_count)
    head_outputs = []
    for sub_head in range(QPK):
        query_head = query_local[:, sub_head * head_size : (sub_head + 1) * head_size]
        column_tiles = []
        for first_row in range(0, row_count, query_block):
            query_tile = query_head[first_row : first_row + query_block]
            low_key = max(0, first_row - WINDOW + 1)
            high_key = first_row + query_block
            halo_need = max(0, WINDOW - 1 - first_row)
            query_pos = first_row + lax.broadcasted_iota(jnp.int32, (query_block, 1), 0)
            local_pos = low_key + lax.broadcasted_iota(jnp.int32, (1, high_key - low_key), 1)
            local_valid = (local_pos <= query_pos) & (query_pos - local_pos < WINDOW)
            local_keys = local_pair[0, low_key:high_key]
            local_values = local_pair[1, low_key:high_key]
            local_scores = masked_scores(query_tile, local_keys, local_valid)
            halo_pos = lax.broadcasted_iota(jnp.int32, (1, halo_need), 1) - halo_need
            halo_valid = (query_pos - halo_pos < WINDOW) & jnp.logical_not(opening)
            halo_keys = borrowed[0, borrowed_rows - halo_need :]
            halo_values = borrowed[1, borrowed_rows - halo_need :]
            halo_scores = masked_scores(query_tile, halo_keys, halo_valid)
            all_scores = jnp.concatenate([halo_scores, local_scores], axis=1)
            all_values = jnp.concatenate([halo_values, local_values], axis=0)
            context = joined_context(all_scores, all_values)
            column_tiles.append(context.astype(jnp.bfloat16))
        head_outputs.append(jnp.concatenate(column_tiles, axis=0))
    attended = jnp.concatenate(head_outputs, axis=1)
    return attended.reshape(1, 1, row_count, QPK * head_size)


def solution(mesh):
    in_specs = (P("seq", "mp", None, None), P("seq", "mp", None, None), P("seq", "mp", None, None))
    out_specs = P("seq", "mp", None, None)
    return jax.shard_map(
        per_device, mesh=mesh, in_specs=in_specs, out_specs=out_specs, check_vma=False
    )
```

profile of v0, /device:TPU:4, one launch (start us, length us, event | category | flops | bytes accessed | tf_op | source)
XLA Modules:
  0.0 47.2 jit_solution(16105123148899370447)
XLA Ops:
  0.0 1.2 %pad_maximum_fusion = bf16[2,1280,128]{2,1,0:T(8,128)(2,1)S(1)} fusion(bf16[1,1280,128]{2,1,0:T(8,128)(2,1)} %bitcast.57, bf16[1,1280,128]{2,1,0:T(8,128)(2,1)} %bitcast.61), kind=kLoop, calls=%fused_computation.54 | loop fusion | flops 327680 | bytes 1310720 | tf_op jit(solution)/shard_map/stack | solution.py:51
  1.2 3.4 %collective-permute-start = (bf16[2,1280,128]{2,1,0:T(8,128)(2,1)S(1)}, bf16[2,1280,128]{2,1,0:T(8,128)(2,1)S(1)}, u32[]{:S(2)}, u32[]{:S(2)}) collective-permute-start(bf16[2,1280,128]{2,1,0:T(8,128)(2,1)S(1)} %pad_maximum_fusion), channel_id=1, source_target_pairs={{0,8},{8,16},{16,24},{1,9},{9,17},{17,25},{2,10},{10,18},{18,26},{... | collective-permute-start | bytes 1966088 | tf_op jit(solution)/shard_map/ppermute | solution.py:17
  5.2 0.9 %slice_bitcast_fusion.4 = bf16[640,128]{1,0:T(8,128)(2,1)S(1)} fusion(bf16[1,1280,128]{2,1,0:T(8,128)(2,1)} %bitcast.58), kind=kLoop, calls=%fused_computation.63 | loop fusion | bytes 327680 | tf_op jit(solution)/shard_map/squeeze | solution.py:75
  6.1 2.7 %fusion.81 = (f32[640]{0:T(1024)S(1)}, f32[640,640]{0,1:T(8,128)}) fusion(bf16[1,1280,128]{2,1,0:T(8,128)(2,1)} %bitcast.62, bf16[1280,256]{1,0:T(8,128)(2,1)} %bitcast.64), kind=kOutput, calls=%fused_computation.93 | convolution fusion | flops 107724160 | bytes 1968640 | tf_op jit(solution)/shard_map/qd,kd->qk/dot_general | solution.py:29
  8.8 1.3 %fusion.77 = (f32[640]{0:T(1024)S(1)}, f32[640,640]{0,1:T(8,128)S(1)}) fusion(bf16[1,1280,128]{2,1,0:T(8,128)(2,1)S(1)} %bitcast.63, bf16[1280,256]{1,0:T(8,128)(2,1)} %bitcast.65), kind=kOutput, calls=%fused_computation.89 | convolution fusion | flops 107724160 | bytes 1968640 | tf_op jit(solution)/shard_map/qd,kd->qk/dot_general | solution.py:29
  10.7 3.8 %fusion.79 = (f32[640]{0:T(1024)S(1)}, f32[640,1280]{1,0:T(8,128)}) fusion(bf16[1,1,1280,128]{3,2,1,0:T(8,128)(2,1)S(1)} %copy-done.6, bf16[1280,256]{1,0:T(8,128)(2,1)} %bitcast.66, s32[640]{0:T(1024)S(1)} %iota_add_fusion), kind=kOutput, calls=%fused_computation.91 | convolution fusion | flops 215448960 | bytes 3773440 | tf_op jit(solution)/shard_map/qd,kd->qk/dot_general | solution.py:29
  14.5 2.8 %fusion.75 = (f32[640]{0:T(1024)S(1)}, f32[640,1280]{1,0:T(8,128)}) fusion(bf16[1,1,1280,128]{3,2,1,0:T(8,128)(2,1)S(1)} %copy-done.6, bf16[1280,256]{1,0:T(8,128)(2,1)S(1)} %bitcast.67, s32[640]{0:T(1024)S(1)} %iota_add_fusion), kind=kOutput, calls=%fused_computation.87 | convolution fusion | flops 215448960 | bytes 3774976 | tf_op jit(solution)/shard_map/qd,kd->qk/dot_general | solution.py:29
  17.4 3.1 %collective-permute-done = bf16[2,1280,128]{2,1,0:T(8,128)(2,1)S(1)} collective-permute-done((bf16[2,1280,128]{2,1,0:T(8,128)(2,1)S(1)}, bf16[2,1280,128]{2,1,0:T(8,128)(2,1)S(1)}, u32[]{:S(2)}, u32[]{:S(2)}) %collective-permute-start) | collective-permute-done | bytes 655392 | tf_op jit(solution)/shard_map/ppermute | solution.py:17
  20.6 2.4 %fusion.80 = (f32[640]{0:T(1024)S(1)}, f32[640,1023]{0,1:T(8,128)}) fusion(bf16[1280,256]{1,0:T(8,128)(2,1)S(1)} %bitcast.68, bf16[2,1280,128]{2,1,0:T(8,128)(2,1)S(1)} %broadcast_select_fusion, pred[]{:T(512)S(6)} %not.2, s32[1023]{0:T(1024)S(1)} %copy-done.9), kind=kOutput, calls=%fused_computation.92 | convolution fusion | flops 171536000 | bytes 3051521 | tf_op jit(solution)/shard_map/qd,kd->qk/dot_general | solution.py:29
  23.1 2.5 %fusion.76 = (f32[640]{0:T(1024)S(1)}, f32[640,1023]{0,1:T(8,128)}) fusion(bf16[1280,256]{1,0:T(8,128)(2,1)S(1)} %bitcast.69, bf16[2,1280,128]{2,1,0:T(8,128)(2,1)S(1)} %broadcast_select_fusion, pred[]{:T(512)S(6)} %not.2, s32[1023]{0:T(1024)S(1)} %copy-done.9), kind=kOutput, calls=%fused_computation.88 | convolution fusion | flops 171536000 | bytes 3051521 | tf_op jit(solution)/shard_map/qd,kd->qk/dot_general | solution.py:29
  25.6 1.3 %fusion.78 = (f32[640]{0:T(1024)S(1)}, f32[640,383]{0,1:T(8,128)}) fusion(bf16[1280,256]{1,0:T(8,128)(2,1)S(1)} %bitcast.70, bf16[2,1280,128]{2,1,0:T(8,128)(2,1)S(1)} %broadcast_select_fusion, pred[]{:T(512)S(6)} %not.2, s32[383]{0:T(512)S(1)} %copy-done.10, s32[640]{0:T(1024)S(1)} %copy-done.8), kind=kOutput, calls=%fused_computation.90 | convolution fusion | flops 64220800 | bytes 1251329 | tf_op jit(solution)/shard_map/qd,kd->qk/dot_general | solution.py:29
  26.9 1.3 %fusion.74 = (f32[640]{0:T(1024)S(1)}, f32[640,383]{0,1:T(8,128)}) fusion(bf16[1280,256]{1,0:T(8,128)(2,1)S(1)} %bitcast.71, bf16[2,1280,128]{2,1,0:T(8,128)(2,1)S(1)} %broadcast_select_fusion, pred[]{:T(512)S(6)} %not.2, s32[383]{0:T(512)S(1)} %copy-done.10, s32[640]{0:T(1024)S(1)} %copy-done.8), kind=kOutput, calls=%fused_computation.86 | convolution fusion | flops 64220800 | bytes 1251329 | tf_op jit(solution)/shard_map/qd,kd->qk/dot_general | solution.py:29
  28.3 1.5 %copy.4 = f32[640,383]{1,0:T(8,128)S(1)} copy(f32[640,383]{0,1:T(8,128)} %get-tuple-element.14) | data formatting | bytes 1960960 | tf_op jit(solution)/shard_map/jit(_where)/select_n | solution.py:32
  29.8 3.1 %fusion.14 = f32[640]{0:T(1024)S(1)} fusion(f32[640,640]{0,1:T(8,128)} %get-tuple-element.20, f32[640,1023]{0,1:T(8,128)} %get-tuple-element.18, f32[640]{0:T(1024)S(1)} %reduce_max.82), kind=kLoop, calls=%fused_computation.22 | loop fusion | flops 3192320 | bytes 4262400 | tf_op jit(solution)/shard_map/reduce_sum | solution.py:38
  33.3 0.9 %fusion.52 = bf16[640,128]{1,0:T(8,128)(2,1)S(1)} fusion(f32[640,640]{0,1:T(8,128)S(1)} %copy-done.4, f32[640,1023]{0,1:T(8,128)S(1)} %copy-done.3, f32[640]{0:T(1024)S(1)} %reduce_max.82, bf16[640,128]{1,0:T(8,128)(2,1)S(1)} %slice_bitcast_fusion.4, bf16[1023,128]{1,0:T(8,128)(2,1)S(1)} %slice_bitcast_fusion, f32[640]{0:T(1024)S(1)} %fusion.14), kind=kOutput, calls=%fused_computation.51 | convolution fusion | flops 276674176 | bytes 4851968 | tf_op jit(solution)/shard_map/dot_general | solution.py:40
  34.2 0.9 %copy-done.2 = f32[640,1023]{0,1:T(8,128)S(1)} copy-done((f32[640,1023]{0,1:T(8,128)S(1)}, f32[640,1023]{0,1:T(8,128)}, u32[]{:S(2)}) %copy-start.2) | copy-done | bytes 2618904
  35.0 0.7 %fusion.10 = f32[640]{0:T(1024)S(1)} fusion(f32[640,640]{0,1:T(8,128)S(1)} %get-tuple-element.12, f32[640,1023]{0,1:T(8,128)S(1)} %copy-done.2, f32[640]{0:T(1024)S(1)} %reduce_max.88), kind=kLoop, calls=%fused_computation.18 | loop fusion | flops 3192320 | bytes 4262400 | tf_op jit(solution)/shard_map/reduce_sum | solution.py:38
  35.8 0.8 %fusion.46 = bf16[640,128]{1,0:T(8,128)(2,1)S(1)} fusion(f32[640,640]{0,1:T(8,128)S(1)} %get-tuple-element.12, f32[640,1023]{0,1:T(8,128)S(1)} %copy-done.2, f32[640]{0:T(1024)S(1)} %reduce_max.88, bf16[640,128]{1,0:T(8,128)(2,1)S(1)} %slice_bitcast_fusion.4, bf16[1023,128]{1,0:T(8,128)(2,1)S(1)} %slice_bitcast_fusion, f32[640]{0:T(1024)S(1)} %fusion.10), kind=kOutput, calls=%fused_computation.49 | convolution fusion | flops 276674176 | bytes 4851968 | tf_op jit(solution)/shard_map/dot_general | solution.py:40
  36.6 1.6 %copy.5 = f32[640,383]{1,0:T(8,128)S(1)} copy(f32[640,383]{0,1:T(8,128)} %get-tuple-element.6) | data formatting | bytes 1960960 | tf_op jit(solution)/shard_map/jit(_where)/select_n | solution.py:32
  38.3 3.4 %fusion.12 = f32[640]{0:T(1024)S(1)} fusion(f32[640,1280]{1,0:T(8,128)} %get-tuple-element.16, f32[640,383]{1,0:T(8,128)S(1)} %copy.4, f32[640]{0:T(1024)S(1)} %reduce_max.85), kind=kLoop, calls=%fused_computation.20 | loop fusion | flops 3192320 | bytes 4262400 | tf_op jit(solution)/shard_map/reduce_sum | solution.py:38
  41.7 1.5 %fusion.40 = bf16[640,128]{1,0:T(8,128)(2,1)S(1)} fusion(f32[640,1280]{1,0:T(8,128)S(1)} %copy-done.1, f32[640,383]{1,0:T(8,128)S(1)} %copy.4, f32[640]{0:T(1024)S(1)} %reduce_max.85, bf16[1280,128]{1,0:T(8,128)(2,1)S(1)} %bitcast.59, bf16[383,128]{1,0:T(8,128)(2,1)S(1)} %slice_bitcast_fusion.8, f32[640]{0:T(1024)S(1)} %fusion.12), kind=kOutput, calls=%fused_computation.47 | convolution fusion | flops 276674176 | bytes 4851968 | tf_op jit(solution)/shard_map/dot_general | solution.py:40
  43.6 1.4 %fusion.8 = f32[640]{0:T(1024)S(1)} fusion(f32[640,1280]{1,0:T(8,128)S(1)} %copy-done, f32[640,383]{1,0:T(8,128)S(1)} %copy.5, f32[640]{0:T(1024)S(1)} %reduce_max.91), kind=kLoop, calls=%fused_computation.16 | loop fusion | flops 3192320 | bytes 4262400 | tf_op jit(solution)/shard_map/reduce_sum | solution.py:38
  45.0 1.3 %fusion.34 = bf16[640,128]{1,0:T(8,128)(2,1)S(1)} fusion(f32[640,1280]{1,0:T(8,128)S(1)} %copy-done, f32[640,383]{1,0:T(8,128)S(1)} %copy.5, f32[640]{0:T(1024)S(1)} %reduce_max.91, bf16[1280,128]{1,0:T(8,128)(2,1)S(1)} %bitcast.60, bf16[383,128]{1,0:T(8,128)(2,1)S(1)} %slice_bitcast_fusion.8, f32[640]{0:T(1024)S(1)} %fusion.8), kind=kOutput, calls=%fused_computation.45 | convolution fusion | flops 276674176 | bytes 4851968 | tf_op jit(solution)/shard_map/dot_general | solution.py:40
  46.3 0.9 %maximum_bitcast_fusion = bf16[1,1,1280,256]{3,2,1,0:T(8,128)(2,1)} fusion(bf16[640,128]{1,0:T(8,128)(2,1)S(1)} %fusion.34, bf16[640,128]{1,0:T(8,128)(2,1)S(1)} %fusion.46, bf16[640,128]{1,0:T(8,128)(2,1)S(1)} %fusion.40, bf16[640,128]{1,0:T(8,128)(2,1)S(1)} %fusion.52), kind=kLoop, calls=%fused_computation.55 | loop fusion | flops 2621440 | bytes 1310720 | tf_op jit(solution)/shard_map/reshape | solution.py:88
  (33 shorter events, 2.2 us)
Async XLA Ops:
  0.0 8.8 %copy-start.6 = (bf16[1,1,1280,128]{3,2,1,0:T(8,128)(2,1)S(1)}, bf16[1,1,1280,128]{3,2,1,0:T(8,128)(2,1)}, u32[]{:S(2)}) copy-start(bf16[1,1,1280,128]{3,2,1,0:T(8,128)(2,1)} %param.4) | copy-start | bytes 983044
  1.2 19.3 %collective-permute-start = (bf16[2,1280,128]{2,1,0:T(8,128)(2,1)S(1)}, bf16[2,1280,128]{2,1,0:T(8,128)(2,1)S(1)}, u32[]{:S(2)}, u32[]{:S(2)}) collective-permute-start(bf16[2,1280,128]{2,1,0:T(8,128)(2,1)S(1)} %pad_maximum_fusion), channel_id=1, source_target_pairs={{0,8},{8,16},{16,24},{1,9},{9,17},{17,25},{2,10},{10,18},{18,26},{... | collective-permute-start | bytes 1966088 | tf_op jit(solution)/shard_map/ppermute | solution.py:17
  6.1 8.4 %copy-start.7 = (s32[640]{0:T(1024)}, s32[640]{0:T(1024)S(1)}, u32[]{:S(2)}) copy-start(s32[640]{0:T(1024)S(1)} %iota_add_fusion) | copy-start | bytes 7684
  10.7 3.8 %copy-start.11 = (bf16[1,1,1280,256]{3,2,1,0:T(8,128)(2,1)S(1)}, bf16[1,1,1280,256]{3,2,1,0:T(8,128)(2,1)}, u32[]{:S(2)}) copy-start(bf16[1,1,1280,256]{3,2,1,0:T(8,128)(2,1)} %param.3) | copy-start | bytes 1966084
  14.5 6.1 %copy-start.9 = (s32[1023]{0:T(1024)S(1)}, s32[1023]{0:T(1024)}, u32[]{:S(2)}) copy-start(s32[1023]{0:T(1024)} %iota_add_fusion.1) | copy-start | bytes 12280
  23.1 2.5 %copy-start.8 = (s32[640]{0:T(1024)S(1)}, s32[640]{0:T(1024)}, u32[]{:S(2)}) copy-start(s32[640]{0:T(1024)} %copy-done.7) | copy-start | bytes 7684
  23.1 2.5 %copy-start.10 = (s32[383]{0:T(512)S(1)}, s32[383]{0:T(512)}, u32[]{:S(2)}) copy-start(s32[383]{0:T(512)} %iota_add_fusion.2) | copy-start | bytes 4600
  29.8 3.2 %copy-start.3 = (f32[640,1023]{0,1:T(8,128)S(1)}, f32[640,1023]{0,1:T(8,128)}, u32[]{:S(2)}) copy-start(f32[640,1023]{0,1:T(8,128)} %get-tuple-element.18) | copy-start | bytes 7856644
  29.8 3.5 %copy-start.4 = (f32[640,640]{0,1:T(8,128)S(1)}, f32[640,640]{0,1:T(8,128)}, u32[]{:S(2)}) copy-start(f32[640,640]{0,1:T(8,128)} %get-tuple-element.20) | copy-start | bytes 4915204
  33.3 1.7 %copy-start.2 = (f32[640,1023]{0,1:T(8,128)S(1)}, f32[640,1023]{0,1:T(8,128)}, u32[]{:S(2)}) copy-start(f32[640,1023]{0,1:T(8,128)} %get-tuple-element.10) | copy-start | bytes 7856644
  36.6 5.0 %copy-start.5 = (bf16[1,1,1280,128]{3,2,1,0:T(8,128)(2,1)S(1)}, bf16[1,1,1280,128]{3,2,1,0:T(8,128)(2,1)}, u32[]{:S(2)}) copy-start(bf16[1,1,1280,128]{3,2,1,0:T(8,128)(2,1)} %param.5) | copy-start | bytes 983044
  38.2 3.4 %copy-start.1 = (f32[640,1280]{1,0:T(8,128)S(1)}, f32[640,1280]{1,0:T(8,128)}, u32[]{:S(2)}) copy-start(f32[640,1280]{1,0:T(8,128)} %get-tuple-element.16) | copy-start | bytes 9830404
  41.6 1.9 %copy-start = (f32[640,1280]{1,0:T(8,128)S(1)}, f32[640,1280]{1,0:T(8,128)}, u32[]{:S(2)}) copy-start(f32[640,1280]{1,0:T(8,128)} %get-tuple-element.8) | copy-start | bytes 9830404
where the time goes:
time: 47.6 us; the launch traced here: 47.2 us
  matrix products  22.7 us (48%)
  other arithmetic  12 us (25%)
  local copies, waits for them, and re-layouts  5.81 us (12%)
  starting transfers between devices  3.4 us (7%)
  waiting for transfers between devices  3.09 us (6%)
    dot_general x8, matrix products, masked_scores(): jnp.einsum('qd,kd->qk', query_tile, key_tile, preferred_element_type=jnp....  18.2 us
    reduce_sum x4, other arithmetic, joined_context(): row_total = jnp.sum(probable, axis=1, keepdims=True)  8.62 us
    dot_general x4, matrix products, joined_context(): jnp.dot(weights, value_tile, preferred_element_type=jnp.float32) / row_total  4.51 us
    ppermute x1, starting transfers between devices, passed_along(): return lax.ppermute(block, axis, route)  3.4 us
    select_n x2, local copies, waits for them, and re-layouts, masked_scores(): return jnp.where(valid, raw, -jnp.inf)  3.11 us
    ppermute x1, waiting for transfers between devices, passed_along(): return lax.ppermute(block, axis, route)  3.09 us
    unnamed x24, local copies, waits for them, and re-layouts  1.68 us
    another operation x1, other arithmetic, per_device(): local_pair = jnp.stack([key_rows[0, 0], value_rows[0, 0]])  1.18 us
  transfers between devices with their start and end apart: 1, of which 1 were waited for; matrix products, arithmetic and copies ran while one was open for 27% of the time, Pallas kernels for 0%

commit v1 on v0

v1 whole, which is shorter than its diff:
```python
import functools
import math

import jax
import jax.numpy as jnp
from jax import lax
from jax.experimental import pallas as pl
from jax.experimental.pallas import tpu as pltpu
from jax.sharding import PartitionSpec as P

KVH = 8
QPK = 2
WINDOW = 1024
TILE = 256
LOG2_SCALE = 168.0 ** (-0.5) * math.log2(math.e)
LOWEST = -1e30


def attention_kernel(
    seq_count, mp_count, q_hbm, k_hbm, v_hbm, o_hbm, q_rows, keys, values, o_rows, in_sem, out_sem, send_sem, recv_sem
):
    rows = q_hbm.shape[2]
    head = k_hbm.shape[3]
    blocks_here = mp_count // KVH
    total = seq_count * blocks_here
    chunks = WINDOW // TILE
    q_blocks = rows // TILE
    mp_index = lax.axis_index("mp")
    kv_head = mp_index % KVH
    group = lax.axis_index("seq") * blocks_here + mp_index // KVH
    opening = group == 0
    closing = group == total - 1

    def device_of(number):
        return (number // blocks_here, (number % blocks_here) * KVH + kv_head)

    following = device_of((group + 1) % total)
    previous = device_of((group + total - 1) % total)

    barrier = pltpu.get_barrier_semaphore()

    @pl.when(jnp.logical_not(opening))
    def _():
        pl.semaphore_signal(barrier, inc=1, device_id=previous, device_id_type=pl.DeviceIdType.MESH)

    loads = [
        pltpu.make_async_copy(k_hbm.at[0, 0], keys.at[pl.ds(WINDOW, rows)], in_sem.at[0]),
        pltpu.make_async_copy(q_hbm.at[0, 0], q_rows, in_sem.at[1]),
        pltpu.make_async_copy(v_hbm.at[0, 0], values.at[pl.ds(WINDOW, rows)], in_sem.at[2]),
    ]
    for load in loads:
        load.start()

    def halo_copies(chunk):
        made = []
        for which, (source, target) in enumerate(((k_hbm, keys), (v_hbm, values))):
            made.append(
                pltpu.make_async_remote_copy(
                    src_ref=source.at[0, 0, pl.ds(rows - WINDOW + chunk * TILE, TILE)],
                    dst_ref=target.at[pl.ds(chunk * TILE, TILE)],
                    send_sem=send_sem.at[chunk, which],
                    recv_sem=recv_sem.at[chunk, which],
                    device_id=following,
                    device_id_type=pl.DeviceIdType.MESH,
                )
            )
        return made

    copies = [halo_copies(chunk) for chunk in range(chunks)]

    @pl.when(jnp.logical_not(closing))
    def _():
        pl.semaphore_wait(barrier, 1)
        for chunk in reversed(range(chunks)):
            for copy in copies[chunk]:
                copy.start()

    @pl.when(opening)
    def _():
        keys[0:WINDOW, :] = jnp.zeros((WINDOW, head), jnp.bfloat16)
        values[0:WINDOW, :] = jnp.zeros((WINDOW, head), jnp.bfloat16)

    halo_bias = jnp.where(opening, LOWEST, 0.0).astype(jnp.float32)

    def arrive(chunk):
        @pl.when(jnp.logical_not(opening))
        def _():
            for copy in copies[chunk]:
                copy.wait_recv()

    row_index = lax.broadcasted_iota(jnp.int32, (TILE, TILE), 0)
    column_index = lax.broadcasted_iota(jnp.int32, (TILE, TILE), 1)

    def part(block, sub_head, first, last):
        query = q_rows[block * TILE : (block + 1) * TILE, sub_head * head : (sub_head + 1) * head]
        tiles = []
        for step in range(first, last):
            place = (block + step) * TILE
            raw = lax.dot_general(
                query, keys[place : place + TILE, :], (((1,), (1,)), ((), ())), preferred_element_type=jnp.float32
            )
            if step == 0:
                raw = jnp.where(column_index > row_index, raw, LOWEST)
            if step == chunks:
                raw = jnp.where(column_index <= row_index, raw, LOWEST)
            tiles.append(raw)
        halo_tiles = min(max(chunks - block - first, 0), last - first)
        top = None
        if halo_tiles > 0:
            top = functools.reduce(jnp.maximum, tiles[:halo_tiles])
            top = jnp.max(top, axis=1, keepdims=True) + halo_bias
        if halo_tiles < len(tiles):
            local_top = functools.reduce(jnp.maximum, tiles[halo_tiles:])
            local_top = jnp.max(local_top, axis=1, keepdims=True)
            top = local_top if top is None else jnp.maximum(top, local_top)
        return tiles, halo_tiles, top

    def weigh(block, first, tiles, halo_tiles, top):
        shift = top * LOG2_SCALE
        halo_shift = shift - halo_bias
        lane_total = None
        gathered = None
        for number, raw in enumerate(tiles):
            probable = jnp.exp2(raw * LOG2_SCALE - (halo_shift if number < halo_tiles else shift))
            lane_total = probable if lane_total is None else lane_total + probable
            place = (block + first + number) * TILE
            term = jnp.dot(
                probable.astype(jnp.bfloat16), values[place : place + TILE, :], preferred_element_type=jnp.float32
            )
            gathered = term if gathered is None else gathered + term
        return jnp.sum(lane_total, axis=1, keepdims=True), gathered

    def store_out(block):
        return pltpu.make_async_copy(
            o_rows.at[pl.ds(block * TILE, TILE)], o_hbm.at[0, 0, pl.ds(block * TILE, TILE)], out_sem.at[block]
        )

    def finish(block, sub_head, row_total, gathered):
        o_rows[block * TILE : (block + 1) * TILE, sub_head * head : (sub_head + 1) * head] = (
            gathered / row_total
        ).astype(jnp.bfloat16)

    for load in loads:
        load.wait()

    held = []
    for block in reversed(range(q_blocks)):
        if 0 < block < chunks:
            arrive(block)
        for sub_head in range(QPK):
            first = 1 if block == 0 else 0
            tiles, halo_tiles, top = part(block, sub_head, first, chunks + 1)
            row_total, gathered = weigh(block, first, tiles, halo_tiles, top)
            if block == 0:
                held.append((top, row_total, gathered))
            else:
                finish(block, sub_head, row_total, gathered)
        if block > 0:
            store_out(block).start()
    arrive(0)
    for sub_head in range(QPK):
        top, row_total, gathered = held[sub_head]
        tiles, halo_tiles, edge_top = part(0, sub_head, 0, 1)
        new_top = jnp.maximum(top, edge_top)
        keep = jnp.exp2((top - new_top) * LOG2_SCALE)
        edge_total, edge_gathered = weigh(0, 0, tiles, halo_tiles, new_top)
        finish(0, sub_head, row_total * keep + edge_total, gathered * keep + edge_gathered)
    store_out(0).start()

    @pl.when(jnp.logical_not(closing))
    def _():
        for chunk in reversed(range(chunks)):
            for copy in copies[chunk]:
                copy.wait_send()

    for block in reversed(range(q_blocks)):
        store_out(block).wait()


def solution(mesh):
    seq_count = mesh.shape["seq"]
    mp_count = mesh.shape["mp"]

    def per_device(queries, key_rows, value_rows):
        rows = queries.shape[2]
        head = key_rows.shape[3]
        span = rows + WINDOW
        return pl.pallas_call(
            functools.partial(attention_kernel, seq_count, mp_count),
            out_shape=jax.ShapeDtypeStruct(queries.shape, jnp.bfloat16),
            in_specs=[pl.BlockSpec(memory_space=pltpu.HBM)] * 3,
            out_specs=pl.BlockSpec(memory_space=pl.ANY),
            scratch_shapes=[
                pltpu.VMEM((rows, QPK * head), jnp.bfloat16),
                pltpu.VMEM((span, head), jnp.bfloat16),
                pltpu.VMEM((span, head), jnp.bfloat16),
                pltpu.VMEM((rows, QPK * head), jnp.bfloat16),
                pltpu.SemaphoreType.DMA((3,)),
                pltpu.SemaphoreType.DMA((rows // TILE,)),
                pltpu.SemaphoreType.DMA((WINDOW // TILE, 2)),
                pltpu.SemaphoreType.DMA((WINDOW // TILE, 2)),
            ],
            compiler_params=pltpu.CompilerParams(
                collective_id=0, has_side_effects=True, vmem_limit_bytes=32 * 1024 * 1024
            ),
            cost_estimate=pl.CostEstimate(
                flops=4 * QPK * rows * (WINDOW + TILE) * head,
                bytes_accessed=6 * rows * QPK * head,
                transcendentals=QPK * rows * (WINDOW + TILE),
            ),
        )(queries, key_rows, value_rows)

    spec = P("seq", "mp", None, None)
    return jax.shard_map(per_device, mesh=mesh, in_specs=(spec, spec, spec), out_specs=spec, check_vma=False)
```

time: 47.6 us -> 20.7 us (0.43)
  matrix products: 22.7 us -> 0 us
  Pallas kernels: 0 us -> 16.5 us
  other arithmetic: 12 us -> 0 us
  starting transfers between devices: 3.4 us -> 0 us
  waiting for transfers between devices: 3.09 us -> 0 us
  local copies, waits for them, and re-layouts: 5.81 us -> 3.87 us
    dot_general x12 -> x0, matrix products: 22.7 us -> none  [the longest x8 18.2 us: masked_scores(): jnp.einsum('qd,kd->qk', query_tile, key_tile, preferred_element_type=jnp....]
    pallas_call x0 -> x1, Pallas kernels: none -> 16.5 us  [per_device(): pl.pallas_call(functools.partial(attention_kernel, seq_count, mp_count),...]
    reduce_sum x4 -> x0, other arithmetic: 8.62 us -> none  [joined_context(): row_total = jnp.sum(probable, axis=1, keepdims=True)]
    ppermute x1 -> x0, starting transfers between devices: 3.4 us -> none  [passed_along(): return lax.ppermute(block, axis, route)]
    select_n x2 -> x0, local copies, waits for them, and re-layouts: 3.11 us -> none  [masked_scores(): return jnp.where(valid, raw, -jnp.inf)]
    ppermute x1 -> x0, waiting for transfers between devices: 3.09 us -> none  [passed_along(): return lax.ppermute(block, axis, route)]
    unnamed x24 -> x7, local copies, waits for them, and re-layouts: 1.68 us -> 3.87 us
    another operation x1 -> x0, other arithmetic: 1.18 us -> none  [per_device(): local_pair = jnp.stack([key_rows[0, 0], value_rows[0, 0]])]
  transfers between devices with their start and end apart: 1 -> 0, of which waited for: 1 -> 0; matrix products, arithmetic and copies ran while one was open for 27% -> 0% of each run, Pallas kernels for 0% -> 0%
where the time goes in v1:
time: 20.7 us; the launch traced here: 20.4 us
  Pallas kernels  16.5 us (80%)
  local copies, waits for them, and re-layouts  3.87 us (19%)
    pallas_call x1, Pallas kernels, per_device(): pl.pallas_call(functools.partial(attention_kernel, seq_count, mp_count),...  16.5 us
    unnamed x7, local copies, waits for them, and re-layouts  3.87 us

profile of v1, /device:TPU:4, one launch (start us, length us, event | category | flops | bytes accessed | tf_op | source)
XLA Modules:
  0.0 20.4 jit_solution(81834376410701125)
XLA Ops:
  0.0 0.0 copy-start
  0.0 1.1 %copy-done = bf16[1,1,1280,256]{3,2,1,0:T(8,128)(2,1)S(1)} copy-done((bf16[1,1,1280,256]{3,2,1,0:T(8,128)(2,1)S(1)}, bf16[1,1,1280,256]{3,2,1,0:T(8,128)(2,1)}, u32[]{:S(2)}) %copy-start) | copy-done | bytes 655384
  1.1 0.0 copy-start.1
  1.1 1.0 %copy-done.1 = bf16[1,1,1280,128]{3,2,1,0:T(8,128)(2,1)S(1)} copy-done((bf16[1,1,1280,128]{3,2,1,0:T(8,128)(2,1)S(1)}, bf16[1,1,1280,128]{3,2,1,0:T(8,128)(2,1)}, u32[]{:S(2)}) %copy-start.1) | copy-done | bytes 327704
  2.1 0.0 copy-start.2
  2.1 1.0 %copy-done.2 = bf16[1,1,1280,128]{3,2,1,0:T(8,128)(2,1)S(1)} copy-done((bf16[1,1,1280,128]{3,2,1,0:T(8,128)(2,1)S(1)}, bf16[1,1,1280,128]{3,2,1,0:T(8,128)(2,1)}, u32[]{:S(2)}) %copy-start.2) | copy-done | bytes 327704
  3.0 16.5 %shard_map.37 = bf16[1,1,1280,256]{3,2,1,0:T(8,128)(2,1)S(1)} custom-call(bf16[1,1,1280,256]{3,2,1,0:T(8,128)(2,1)S(1)} %copy-done, bf16[1,1,1280,128]{3,2,1,0:T(8,128)(2,1)S(1)} %copy-done.1, bf16[1,1,1280,128]{3,2,1,0:T(8,128)(2,1)S(1)} %copy-done.2), custom_call_target="tpu_custom_call" | custom-call | flops 1677721600 | bytes 1966080 | tf_op jit(solution)/shard_map/pallas_call | solution.py:188
  19.6 0.8 %copy.5 = bf16[1,1,1280,256]{3,2,1,0:T(8,128)(2,1)} copy(bf16[1,1,1280,256]{3,2,1,0:T(8,128)(2,1)S(1)} %shard_map.37) | data formatting | bytes 1310720
Async XLA Ops:
  0.0 1.1 %copy-start = (bf16[1,1,1280,256]{3,2,1,0:T(8,128)(2,1)S(1)}, bf16[1,1,1280,256]{3,2,1,0:T(8,128)(2,1)}, u32[]{:S(2)}) copy-start(bf16[1,1,1280,256]{3,2,1,0:T(8,128)(2,1)} %q_hbm.1) | copy-start | bytes 1966084
  1.1 1.0 %copy-start.1 = (bf16[1,1,1280,128]{3,2,1,0:T(8,128)(2,1)S(1)}, bf16[1,1,1280,128]{3,2,1,0:T(8,128)(2,1)}, u32[]{:S(2)}) copy-start(bf16[1,1,1280,128]{3,2,1,0:T(8,128)(2,1)} %k_hbm.1) | copy-start | bytes 983044
  2.1 1.0 %copy-start.2 = (bf16[1,1,1280,128]{3,2,1,0:T(8,128)(2,1)S(1)}, bf16[1,1,1280,128]{3,2,1,0:T(8,128)(2,1)}, u32[]{:S(2)}) copy-start(bf16[1,1,1280,128]{3,2,1,0:T(8,128)(2,1)} %v_hbm.1) | copy-start | bytes 983044

commit v2 on v1

--- a/solution.py
+++ b/solution.py
@@ -12,12 +12,14 @@
 QPK = 2
 WINDOW = 1024
 TILE = 256
+PIECE = 128
+IN_FLIGHT = 3
 LOG2_SCALE = 168.0 ** (-0.5) * math.log2(math.e)
 LOWEST = -1e30
 
 
 def attention_kernel(
-    seq_count, mp_count, q_hbm, k_hbm, v_hbm, o_hbm, q_rows, keys, values, o_rows, in_sem, out_sem, send_sem, recv_sem
+    seq_count, mp_count, q_hbm, k_hbm, v_hbm, o_rows, q_rows, keys, values, in_sem, send_sem, recv_sem
 ):
     rows = q_hbm.shape[2]
     head = k_hbm.shape[3]
@@ -51,29 +53,40 @@
     for load in loads:
         load.start()
 
-    def halo_copies(chunk):
+    def halo_copies(piece):
+        first = WINDOW - (piece + 1) * PIECE
         made = []
         for which, (source, target) in enumerate(((k_hbm, keys), (v_hbm, values))):
             made.append(
                 pltpu.make_async_remote_copy(
-                    src_ref=source.at[0, 0, pl.ds(rows - WINDOW + chunk * TILE, TILE)],
-                    dst_ref=target.at[pl.ds(chunk * TILE, TILE)],
-                    send_sem=send_sem.at[chunk, which],
-                    recv_sem=recv_sem.at[chunk, which],
+                    src_ref=source.at[0, 0, pl.ds(rows - WINDOW + first, PIECE)],
+                    dst_ref=target.at[pl.ds(first, PIECE)],
+                    send_sem=send_sem.at[piece, which],
+                    recv_sem=recv_sem.at[piece, which],
                     device_id=following,
                     device_id_type=pl.DeviceIdType.MESH,
                 )
             )
         return made
 
-    copies = [halo_copies(chunk) for chunk in range(chunks)]
+    pieces = WINDOW // PIECE
+    copies = [halo_copies(piece) for piece in range(pieces)]
 
     @pl.when(jnp.logical_not(closing))
     def _():
         pl.semaphore_wait(barrier, 1)
-        for chunk in reversed(range(chunks)):
-            for copy in copies[chunk]:
+        for piece in range(min(IN_FLIGHT, pieces)):
+            for copy in copies[piece]:
                 copy.start()
+
+    def sent(piece):
+        @pl.when(jnp.logical_not(closing))
+        def _():
+            for copy in copies[piece]:
+                copy.wait_send()
+            if piece + IN_FLIGHT < pieces:
+                for copy in copies[piece + IN_FLIGHT]:
+                    copy.start()
 
     @pl.when(opening)
     def _():
@@ -83,10 +96,14 @@
     halo_bias = jnp.where(opening, LOWEST, 0.0).astype(jnp.float32)
 
     def arrive(chunk):
-        @pl.when(jnp.logical_not(opening))
-        def _():
-            for copy in copies[chunk]:
-                copy.wait_recv()
+        per_chunk = TILE // PIECE
+        for piece in range((chunks - 1 - chunk) * per_chunk, (chunks - chunk) * per_chunk):
+            sent(piece)
+
+            @pl.when(jnp.logical_not(opening))
+            def _():
+                for copy in copies[piece]:
+                    copy.wait_recv()
 
     row_index = lax.broadcasted_iota(jnp.int32, (TILE, TILE), 0)
     column_index = lax.broadcasted_iota(jnp.int32, (TILE, TILE), 1)
@@ -130,13 +147,8 @@
             gathered = term if gathered is None else gathered + term
         return jnp.sum(lane_total, axis=1, keepdims=True), gathered
 
-    def store_out(block):
-        return pltpu.make_async_copy(
-            o_rows.at[pl.ds(block * TILE, TILE)], o_hbm.at[0, 0, pl.ds(block * TILE, TILE)], out_sem.at[block]
-        )
-
     def finish(block, sub_head, row_total, gathered):
-        o_rows[block * TILE : (block + 1) * TILE, sub_head * head : (sub_head + 1) * head] = (
+        o_rows[0, 0, block * TILE : (block + 1) * TILE, sub_head * head : (sub_head + 1) * head] = (
             gathered / row_total
         ).astype(jnp.bfloat16)
 
@@ -155,8 +167,6 @@
                 held.append((top, row_total, gathered))
             else:
                 finish(block, sub_head, row_total, gathered)
-        if block > 0:
-            store_out(block).start()
     arrive(0)
     for sub_head in range(QPK):
         top, row_total, gathered = held[sub_head]
@@ -165,16 +175,6 @@
         keep = jnp.exp2((top - new_top) * LOG2_SCALE)
         edge_total, edge_gathered = weigh(0, 0, tiles, halo_tiles, new_top)
         finish(0, sub_head, row_total * keep + edge_total, gathered * keep + edge_gathered)
-    store_out(0).start()
-
-    @pl.when(jnp.logical_not(closing))
-    def _():
-        for chunk in reversed(range(chunks)):
-            for copy in copies[chunk]:
-                copy.wait_send()
-
-    for block in reversed(range(q_blocks)):
-        store_out(block).wait()
 
 
 def solution(mesh):
@@ -189,16 +189,14 @@
             functools.partial(attention_kernel, seq_count, mp_count),
             out_shape=jax.ShapeDtypeStruct(queries.shape, jnp.bfloat16),
             in_specs=[pl.BlockSpec(memory_space=pltpu.HBM)] * 3,
-            out_specs=pl.BlockSpec(memory_space=pl.ANY),
+            out_specs=pl.BlockSpec(memory_space=pltpu.VMEM),
             scratch_shapes=[
                 pltpu.VMEM((rows, QPK * head), jnp.bfloat16),
                 pltpu.VMEM((span, head), jnp.bfloat16),
                 pltpu.VMEM((span, head), jnp.bfloat16),
-                pltpu.VMEM((rows, QPK * head), jnp.bfloat16),
                 pltpu.SemaphoreType.DMA((3,)),
-                pltpu.SemaphoreType.DMA((rows // TILE,)),
-                pltpu.SemaphoreType.DMA((WINDOW // TILE, 2)),
-                pltpu.SemaphoreType.DMA((WINDOW // TILE, 2)),
+                pltpu.SemaphoreType.DMA((WINDOW // PIECE, 2)),
+                pltpu.SemaphoreType.DMA((WINDOW // PIECE, 2)),
             ],
             compiler_params=pltpu.CompilerParams(
                 collective_id=0, has_side_effects=True, vmem_limit_bytes=32 * 1024 * 1024
@@ -208,7 +206,7 @@
                 bytes_accessed=6 * rows * QPK * head,
                 transcendentals=QPK * rows * (WINDOW + TILE),
             ),
-        )(queries, key_rows, value_rows)
+        )(*[pltpu.with_memory_space_constraint(x, pltpu.HBM) for x in (queries, key_rows, value_rows)])
 
     spec = P("seq", "mp", None, None)
     return jax.shard_map(per_device, mesh=mesh, in_specs=(spec, spec, spec), out_specs=spec, check_vma=False)

time: 20.7 us -> 17.3 us (0.84)
  local copies, waits for them, and re-layouts: 3.87 us -> 0.84 us
    unnamed x7 -> x1, local copies, waits for them, and re-layouts: 3.87 us -> 0.84 us
    pallas_call x1, Pallas kernels: 16.5 us -> 16.3 us  [per_device(): pl.pallas_call(functools.partial(attention_kernel, seq_count, mp_count),...]
where the time goes in v2:
time: 17.3 us; the launch traced here: 17.2 us
  Pallas kernels  16.3 us (94%)
  local copies, waits for them, and re-layouts  0.84 us (5%)
    pallas_call x1, Pallas kernels, per_device(): pl.pallas_call(functools.partial(attention_kernel, seq_count, mp_count),...  16.3 us
    unnamed x1, local copies, waits for them, and re-layouts  0.84 us

profile of v2, /device:TPU:4, one launch (start us, length us, event | category | flops | bytes accessed | tf_op | source)
XLA Modules:
  0.0 17.2 jit_solution(6807773943176811672)
XLA Ops:
  0.0 16.3 %shard_map.37 = bf16[1,1,1280,256]{3,2,1,0:T(8,128)(2,1)S(1)} custom-call(bf16[1,1,1280,256]{3,2,1,0:T(8,128)(2,1)} %q_hbm.1, bf16[1,1,1280,128]{3,2,1,0:T(8,128)(2,1)} %k_hbm.1, bf16[1,1,1280,128]{3,2,1,0:T(8,128)(2,1)} %v_hbm.1), custom_call_target="tpu_custom_call" | custom-call | flops 1677721600 | bytes 1966080 | tf_op jit(solution)/shard_map/pallas_call | solution.py:188
  16.3 0.8 %copy.5 = bf16[1,1,1280,256]{3,2,1,0:T(8,128)(2,1)} copy(bf16[1,1,1280,256]{3,2,1,0:T(8,128)(2,1)S(1)} %shard_map.37) | data formatting | bytes 1310720

commit v3 on v2

--- a/solution.py
+++ b/solution.py
@@ -13,7 +13,7 @@
 WINDOW = 1024
 TILE = 256
 PIECE = 128
-IN_FLIGHT = 3
+IN_FLIGHT = 4
 LOG2_SCALE = 168.0 ** (-0.5) * math.log2(math.e)
 LOWEST = -1e30
 
@@ -105,76 +105,73 @@
                 for copy in copies[piece]:
                     copy.wait_recv()
 
-    row_index = lax.broadcasted_iota(jnp.int32, (TILE, TILE), 0)
-    column_index = lax.broadcasted_iota(jnp.int32, (TILE, TILE), 1)
-
-    def part(block, sub_head, first, last):
-        query = q_rows[block * TILE : (block + 1) * TILE, sub_head * head : (sub_head + 1) * head]
-        tiles = []
-        for step in range(first, last):
-            place = (block + step) * TILE
-            raw = lax.dot_general(
-                query, keys[place : place + TILE, :], (((1,), (1,)), ((), ())), preferred_element_type=jnp.float32
-            )
-            if step == 0:
-                raw = jnp.where(column_index > row_index, raw, LOWEST)
-            if step == chunks:
-                raw = jnp.where(column_index <= row_index, raw, LOWEST)
-            tiles.append(raw)
-        halo_tiles = min(max(chunks - block - first, 0), last - first)
-        top = None
-        if halo_tiles > 0:
-            top = functools.reduce(jnp.maximum, tiles[:halo_tiles])
-            top = jnp.max(top, axis=1, keepdims=True) + halo_bias
-        if halo_tiles < len(tiles):
-            local_top = functools.reduce(jnp.maximum, tiles[halo_tiles:])
-            local_top = jnp.max(local_top, axis=1, keepdims=True)
-            top = local_top if top is None else jnp.maximum(top, local_top)
-        return tiles, halo_tiles, top
-
-    def weigh(block, first, tiles, halo_tiles, top):
-        shift = top * LOG2_SCALE
-        halo_shift = shift - halo_bias
+    stacked = QPK * TILE
+    row_index = lax.broadcasted_iota(jnp.int32, (stacked, TILE), 0) % TILE
+    column_index = lax.broadcasted_iota(jnp.int32, (stacked, TILE), 1)
+
+    def scores_of(query, block, step):
+        place = (block + step) * TILE
+        raw = lax.dot_general(
+            query, keys[place : place + TILE, :], (((1,), (1,)), ((), ())), preferred_element_type=jnp.float32
+        )
+        if step == 0:
+            raw = jnp.where(column_index > row_index, raw, LOWEST)
+        if step == chunks:
+            raw = jnp.where(column_index <= row_index, raw, LOWEST)
+        return raw
+
+    def weighed(tiles, shift):
         lane_total = None
         gathered = None
-        for number, raw in enumerate(tiles):
-            probable = jnp.exp2(raw * LOG2_SCALE - (halo_shift if number < halo_tiles else shift))
+        for place, raw in tiles:
+            probable = jnp.exp2(raw * LOG2_SCALE - shift)
             lane_total = probable if lane_total is None else lane_total + probable
-            place = (block + first + number) * TILE
             term = jnp.dot(
                 probable.astype(jnp.bfloat16), values[place : place + TILE, :], preferred_element_type=jnp.float32
             )
             gathered = term if gathered is None else gathered + term
         return jnp.sum(lane_total, axis=1, keepdims=True), gathered
 
-    def finish(block, sub_head, row_total, gathered):
-        o_rows[0, 0, block * TILE : (block + 1) * TILE, sub_head * head : (sub_head + 1) * head] = (
-            gathered / row_total
-        ).astype(jnp.bfloat16)
+    def stacked_query(block):
+        both = q_rows[block * TILE : (block + 1) * TILE, :]
+        return jnp.concatenate([both[:, part * head : (part + 1) * head] for part in range(QPK)], axis=0)
+
+    def local_part(block):
+        query = stacked_query(block)
+        tiles = [
+            ((block + step) * TILE, scores_of(query, block, step))
+            for step in range(max(chunks - block, 0), chunks + 1)
+        ]
+        top = jnp.max(functools.reduce(jnp.maximum, [raw for _, raw in tiles]), axis=1, keepdims=True)
+        return (top,) + weighed(tiles, top * LOG2_SCALE)
+
+    def with_chunk(state, block, chunk):
+        top, row_total, gathered = state
+        raw = scores_of(stacked_query(block), block, chunk - block)
+        new_top = jnp.maximum(top, jnp.max(raw, axis=1, keepdims=True) + halo_bias)
+        keep = jnp.exp2((top - new_top) * LOG2_SCALE)
+        more_total, more = weighed([(chunk * TILE, raw)], new_top * LOG2_SCALE - halo_bias)
+        return new_top, row_total * keep + more_total, gathered * keep + more
+
+    def finish(block, state):
+        _, row_total, gathered = state
+        done = (gathered / row_total).astype(jnp.bfloat16)
+        for part in range(QPK):
+            o_rows[0, 0, block * TILE : (block + 1) * TILE, part * head : (part + 1) * head] = done[
+                part * TILE : (part + 1) * TILE
+            ]
 
     for load in loads:
         load.wait()
 
-    held = []
-    for block in reversed(range(q_blocks)):
-        if 0 < block < chunks:
-            arrive(block)
-        for sub_head in range(QPK):
-            first = 1 if block == 0 else 0
-            tiles, halo_tiles, top = part(block, sub_head, first, chunks + 1)
-            row_total, gathered = weigh(block, first, tiles, halo_tiles, top)
-            if block == 0:
-                held.append((top, row_total, gathered))
-            else:
-                finish(block, sub_head, row_total, gathered)
-    arrive(0)
-    for sub_head in range(QPK):
-        top, row_total, gathered = held[sub_head]
-        tiles, halo_tiles, edge_top = part(0, sub_head, 0, 1)
-        new_top = jnp.maximum(top, edge_top)
-        keep = jnp.exp2((top - new_top) * LOG2_SCALE)
-        edge_total, edge_gathered = weigh(0, 0, tiles, halo_tiles, new_top)
-        finish(0, sub_head, row_total * keep + edge_total, gathered * keep + edge_gathered)
+    states = [local_part(block) for block in range(q_blocks)]
+    for block in range(chunks, q_blocks):
+        finish(block, states[block])
+    for chunk in reversed(range(chunks)):
+        arrive(chunk)
+        for block in range(chunk + 1):
+            states[block] = with_chunk(states[block], block, chunk)
+        finish(chunk, states[chunk])
 
 
 def solution(mesh):

time: 17.3 us -> 16.6 us (0.960)
  Pallas kernels: 16.3 us -> 15.6 us
    pallas_call x1, Pallas kernels: 16.3 us -> 15.6 us  [per_device(): pl.pallas_call(functools.partial(attention_kernel, seq_count, mp_count),...]
where the time goes in v3:
time: 16.6 us; the launch traced here: 16.4 us
  Pallas kernels  15.6 us (94%)
  local copies, waits for them, and re-layouts  0.84 us (5%)
    pallas_call x1, Pallas kernels, per_device(): pl.pallas_call(functools.partial(attention_kernel, seq_count, mp_count),...  15.6 us
    unnamed x1, local copies, waits for them, and re-layouts  0.84 us

profile of v3, /device:TPU:4, one launch (start us, length us, event | category | flops | bytes accessed | tf_op | source)
XLA Modules:
  0.0 16.4 jit_solution(3532442386431410468)
XLA Ops:
  0.0 15.6 %shard_map.37 = bf16[1,1,1280,256]{3,2,1,0:T(8,128)(2,1)S(1)} custom-call(bf16[1,1,1280,256]{3,2,1,0:T(8,128)(2,1)} %q_hbm.1, bf16[1,1,1280,128]{3,2,1,0:T(8,128)(2,1)} %k_hbm.1, bf16[1,1,1280,128]{3,2,1,0:T(8,128)(2,1)} %v_hbm.1), custom_call_target="tpu_custom_call" | custom-call | flops 1677721600 | bytes 1966080 | tf_op jit(solution)/shard_map/pallas_call | solution.py:185
  15.6 0.8 %copy.5 = bf16[1,1,1280,256]{3,2,1,0:T(8,128)(2,1)} copy(bf16[1,1,1280,256]{3,2,1,0:T(8,128)(2,1)S(1)} %shard_map.37) | data formatting | bytes 1310720

commit v4 on v3

--- a/solution.py
+++ b/solution.py
@@ -13,7 +13,7 @@
 WINDOW = 1024
 TILE = 256
 PIECE = 128
-IN_FLIGHT = 4
+IN_FLIGHT = 5
 LOG2_SCALE = 168.0 ** (-0.5) * math.log2(math.e)
 LOWEST = -1e30
 
@@ -98,7 +98,6 @@
     def arrive(chunk):
         per_chunk = TILE // PIECE
         for piece in range((chunks - 1 - chunk) * per_chunk, (chunks - chunk) * per_chunk):
-            sent(piece)
 
             @pl.when(jnp.logical_not(opening))
             def _():
@@ -164,14 +163,25 @@
     for load in loads:
         load.wait()
 
-    states = [local_part(block) for block in range(q_blocks)]
-    for block in range(chunks, q_blocks):
-        finish(block, states[block])
+    refills = iter(range(pieces))
+    states = [None] * q_blocks
+    for block in reversed(range(q_blocks)):
+        states[block] = local_part(block)
+        if block >= chunks:
+            finish(block, states[block])
+        if block == 2:
+            sent(next(refills))
+    sent(next(refills))
     for chunk in reversed(range(chunks)):
         arrive(chunk)
-        for block in range(chunk + 1):
+        for block in reversed(range(chunk + 1)):
             states[block] = with_chunk(states[block], block, chunk)
-        finish(chunk, states[chunk])
+            if block == chunk:
+                finish(chunk, states[chunk])
+            if chunk == chunks - 1 and block == 2:
+                sent(next(refills))
+    for piece in refills:
+        sent(piece)
 
 
 def solution(mesh):

time: 16.6 us -> 16.6 us (level)
  no operation moved by 1% of the time
where the time goes in v4:
time: 16.6 us; the launch traced here: 16.4 us
  Pallas kernels  15.6 us (94%)
  local copies, waits for them, and re-layouts  0.84 us (5%)
    pallas_call x1, Pallas kernels, per_device(): pl.pallas_call(functools.partial(attention_kernel, seq_count, mp_count),...  15.6 us
    unnamed x1, local copies, waits for them, and re-layouts  0.84 us

profile of v4, /device:TPU:4, one launch (start us, length us, event | category | flops | bytes accessed | tf_op | source)
XLA Modules:
  0.0 16.4 jit_solution(7043404893004246178)
XLA Ops:
  0.0 15.6 %shard_map.37 = bf16[1,1,1280,256]{3,2,1,0:T(8,128)(2,1)S(1)} custom-call(bf16[1,1,1280,256]{3,2,1,0:T(8,128)(2,1)} %q_hbm.1, bf16[1,1,1280,128]{3,2,1,0:T(8,128)(2,1)} %k_hbm.1, bf16[1,1,1280,128]{3,2,1,0:T(8,128)(2,1)} %v_hbm.1), custom_call_target="tpu_custom_call" | custom-call | flops 1677721600 | bytes 1966080 | tf_op jit(solution)/shard_map/pallas_call | solution.py:195
  15.6 0.8 %copy.5 = bf16[1,1,1280,256]{3,2,1,0:T(8,128)(2,1)} copy(bf16[1,1,1280,256]{3,2,1,0:T(8,128)(2,1)S(1)} %shard_map.37) | data formatting | bytes 1310720

commit v5 on v4

--- a/solution.py
+++ b/solution.py
@@ -18,8 +18,44 @@
 LOWEST = -1e30
 
 
+def tile_scores(query, key_tile, window_edge, causal_edge):
+    raw = lax.dot_general(query, key_tile, (((1,), (1,)), ((), ())), preferred_element_type=jnp.float32)
+    row_index = lax.broadcasted_iota(jnp.int32, raw.shape, 0) % TILE
+    column_index = lax.broadcasted_iota(jnp.int32, raw.shape, 1)
+    if window_edge:
+        raw = jnp.where(column_index > row_index, raw, LOWEST)
+    if causal_edge:
+        raw = jnp.where(column_index <= row_index, raw, LOWEST)
+    return raw
+
+
+def weighed(tiles, shift):
+    lane_total = None
+    gathered = None
+    for value_tile, raw in tiles:
+        probable = jnp.exp2(raw * LOG2_SCALE - shift)
+        lane_total = probable if lane_total is None else lane_total + probable
+        term = jnp.dot(probable.astype(jnp.bfloat16), value_tile, preferred_element_type=jnp.float32)
+        gathered = term if gathered is None else gathered + term
+    return jnp.sum(lane_total, axis=1, keepdims=True), gathered
+
+
+def merged(state, raw, value_tile, halo_bias):
+    top, row_total, gathered = state
+    new_top = jnp.maximum(top, jnp.max(raw, axis=1, keepdims=True) + halo_bias)
+    keep = jnp.exp2((top - new_top) * LOG2_SCALE)
+    more_total, more = weighed([(value_tile, raw)], new_top * LOG2_SCALE - halo_bias)
+    return new_top, row_total * keep + more_total, gathered * keep + more
+
+
+def divided(state):
+    _, row_total, gathered = state
+    return (gathered / row_total).astype(jnp.bfloat16)
+
+
 def attention_kernel(
-    seq_count, mp_count, q_hbm, k_hbm, v_hbm, o_rows, q_rows, keys, values, in_sem, send_sem, recv_sem
+    seq_count, mp_count, q_hbm, k_hbm, v_hbm, o_rows, query_out, key_out, value_out, top_out, total_out, gathered_out,
+    q_rows, keys, values, in_sem, send_sem, recv_sem
 ):
     rows = q_hbm.shape[2]
     head = k_hbm.shape[3]
@@ -104,32 +140,9 @@
                 for copy in copies[piece]:
                     copy.wait_recv()
 
-    stacked = QPK * TILE
-    row_index = lax.broadcasted_iota(jnp.int32, (stacked, TILE), 0) % TILE
-    column_index = lax.broadcasted_iota(jnp.int32, (stacked, TILE), 1)
-
     def scores_of(query, block, step):
         place = (block + step) * TILE
-        raw = lax.dot_general(
-            query, keys[place : place + TILE, :], (((1,), (1,)), ((), ())), preferred_element_type=jnp.float32
-        )
-        if step == 0:
-            raw = jnp.where(column_index > row_index, raw, LOWEST)
-        if step == chunks:
-            raw = jnp.where(column_index <= row_index, raw, LOWEST)
-        return raw
-
-    def weighed(tiles, shift):
-        lane_total = None
-        gathered = None
-        for place, raw in tiles:
-            probable = jnp.exp2(raw * LOG2_SCALE - shift)
-            lane_total = probable if lane_total is None else lane_total + probable
-            term = jnp.dot(
-                probable.astype(jnp.bfloat16), values[place : place + TILE, :], preferred_element_type=jnp.float32
-            )
-            gathered = term if gathered is None else gathered + term
-        return jnp.sum(lane_total, axis=1, keepdims=True), gathered
+        return tile_scores(query, keys[place : place + TILE, :], step == 0, step == chunks)
 
     def stacked_query(block):
         both = q_rows[block * TILE : (block + 1) * TILE, :]
@@ -138,27 +151,21 @@
     def local_part(block):
         query = stacked_query(block)
         tiles = [
-            ((block + step) * TILE, scores_of(query, block, step))
+            (values[(block + step) * TILE : (block + step + 1) * TILE, :], scores_of(query, block, step))
             for step in range(max(chunks - block, 0), chunks + 1)
         ]
         top = jnp.max(functools.reduce(jnp.maximum, [raw for _, raw in tiles]), axis=1, keepdims=True)
         return (top,) + weighed(tiles, top * LOG2_SCALE)
 
     def with_chunk(state, block, chunk):
-        top, row_total, gathered = state
-        raw = scores_of(stacked_query(block), block, chunk - block)
-        new_top = jnp.maximum(top, jnp.max(raw, axis=1, keepdims=True) + halo_bias)
-        keep = jnp.exp2((top - new_top) * LOG2_SCALE)
-        more_total, more = weighed([(chunk * TILE, raw)], new_top * LOG2_SCALE - halo_bias)
-        return new_top, row_total * keep + more_total, gathered * keep + more
+        value_tile = values[chunk * TILE : (chunk + 1) * TILE, :]
+        return merged(state, scores_of(stacked_query(block), block, chunk - block), value_tile, halo_bias)
 
     def finish(block, state):
-        _, row_total, gathered = state
-        done = (gathered / row_total).astype(jnp.bfloat16)
+        done = divided(state)
+        place = (block - 1) * TILE
         for part in range(QPK):
-            o_rows[0, 0, block * TILE : (block + 1) * TILE, part * head : (part + 1) * head] = done[
-                part * TILE : (part + 1) * TILE
-            ]
+            o_rows[place : place + TILE, part * head : (part + 1) * head] = done[part * TILE : (part + 1) * TILE]
 
     for load in loads:
         load.wait()
@@ -172,7 +179,7 @@
         if block == 2:
             sent(next(refills))
     sent(next(refills))
-    for chunk in reversed(range(chunks)):
+    for chunk in reversed(range(1, chunks)):
         arrive(chunk)
         for block in reversed(range(chunk + 1)):
             states[block] = with_chunk(states[block], block, chunk)
@@ -180,8 +187,40 @@
                 finish(chunk, states[chunk])
             if chunk == chunks - 1 and block == 2:
                 sent(next(refills))
+    query_out[...] = stacked_query(0)
+    top_out[...], total_out[...], gathered_out[...] = states[0]
+    arrive(0)
+    key_out[...] = keys[0:TILE, :]
+    value_out[...] = values[0:TILE, :]
     for piece in refills:
         sent(piece)
+
+
+def closing_kernel(
+    seq_count, mp_count, done_rows, query, key_tile, value_tile, top, row_total, gathered, o_hbm, first_rows, out_sem
+):
+    head = key_tile.shape[1]
+    later = done_rows.shape[0] // TILE
+    blocks_here = mp_count // KVH
+    group = lax.axis_index("seq") * blocks_here + lax.axis_index("mp") // KVH
+    halo_bias = jnp.where(group == 0, LOWEST, 0.0).astype(jnp.float32)
+    copies = [
+        pltpu.make_async_copy(
+            done_rows.at[pl.ds(block * TILE, TILE)], o_hbm.at[0, 0, pl.ds((block + 1) * TILE, TILE)], out_sem.at[block]
+        )
+        for block in range(later)
+    ]
+    for copy in copies:
+        copy.start()
+    raw = tile_scores(query[...], key_tile[...], True, False)
+    done = divided(merged((top[...], row_total[...], gathered[...]), raw, value_tile[...], halo_bias))
+    for part in range(QPK):
+        first_rows[:, part * head : (part + 1) * head] = done[part * TILE : (part + 1) * TILE]
+    last = pltpu.make_async_copy(first_rows, o_hbm.at[0, 0, pl.ds(0, TILE)], out_sem.at[later])
+    last.start()
+    for copy in copies:
+        copy.wait()
+    last.wait()
 
 
 def solution(mesh):
@@ -192,11 +231,21 @@
         rows = queries.shape[2]
         head = key_rows.shape[3]
         span = rows + WINDOW
-        return pl.pallas_call(
+        stacked = QPK * TILE
+        whole = pl.BlockSpec(memory_space=pltpu.VMEM)
+        held = pl.pallas_call(
             functools.partial(attention_kernel, seq_count, mp_count),
-            out_shape=jax.ShapeDtypeStruct(queries.shape, jnp.bfloat16),
+            out_shape=[
+                jax.ShapeDtypeStruct((rows - TILE, QPK * head), jnp.bfloat16),
+                jax.ShapeDtypeStruct((stacked, head), jnp.bfloat16),
+                jax.ShapeDtypeStruct((TILE, head), jnp.bfloat16),
+                jax.ShapeDtypeStruct((TILE, head), jnp.bfloat16),
+                jax.ShapeDtypeStruct((stacked, 1), jnp.float32),
+                jax.ShapeDtypeStruct((stacked, 1), jnp.float32),
+                jax.ShapeDtypeStruct((stacked, head), jnp.float32),
+            ],
             in_specs=[pl.BlockSpec(memory_space=pltpu.HBM)] * 3,
-            out_specs=pl.BlockSpec(memory_space=pltpu.VMEM),
+            out_specs=[whole] * 7,
             scratch_shapes=[
                 pltpu.VMEM((rows, QPK * head), jnp.bfloat16),
                 pltpu.VMEM((span, head), jnp.bfloat16),
@@ -214,6 +263,17 @@
                 transcendentals=QPK * rows * (WINDOW + TILE),
             ),
         )(*[pltpu.with_memory_space_constraint(x, pltpu.HBM) for x in (queries, key_rows, value_rows)])
+        return pl.pallas_call(
+            functools.partial(closing_kernel, seq_count, mp_count),
+            out_shape=jax.ShapeDtypeStruct(queries.shape, jnp.bfloat16),
+            in_specs=[whole] * 7,
+            out_specs=pl.BlockSpec(memory_space=pltpu.HBM),
+            scratch_shapes=[
+                pltpu.VMEM((TILE, QPK * head), jnp.bfloat16),
+                pltpu.SemaphoreType.DMA((rows // TILE,)),
+            ],
+            compiler_params=pltpu.CompilerParams(vmem_limit_bytes=16 * 1024 * 1024),
+        )(*held)
 
     spec = P("seq", "mp", None, None)
     return jax.shard_map(per_device, mesh=mesh, in_specs=(spec, spec, spec), out_specs=spec, check_vma=False)

time: 16.6 us -> 17.6 us (1.060)
  Pallas kernels: 15.6 us -> 17.5 us
  local copies, waits for them, and re-layouts: 0.84 us -> 0 us
    pallas_call x0 -> x1, Pallas kernels: none -> 2.38 us  [per_device(): pl.pallas_call(functools.partial(closing_kernel, seq_count, mp_count), ou...]
    unnamed x1 -> x0, local copies, waits for them, and re-layouts: 0.84 us -> none
    pallas_call x1, Pallas kernels: 15.6 us -> 15.1 us  [per_device(): pl.pallas_call(functools.partial(attention_kernel, seq_count, mp_count),...]
where the time goes in v5:
time: 17.6 us; the launch traced here: 17.5 us
  Pallas kernels  17.5 us (99%)
    pallas_call x1, Pallas kernels, per_device(): pl.pallas_call(functools.partial(attention_kernel, seq_count, mp_count),...  15.1 us
    pallas_call x1, Pallas kernels, per_device(): pl.pallas_call(functools.partial(closing_kernel, seq_count, mp_count), ou...  2.38 us

profile of v5, /device:TPU:4, one launch (start us, length us, event | category | flops | bytes accessed | tf_op | source)
XLA Modules:
  0.0 17.5 jit_solution(3167294760583565169)
XLA Ops:
  0.0 15.1 %shard_map.37 = (bf16[1024,256]{1,0:T(8,128)(2,1)S(1)}, bf16[512,128]{1,0:T(8,128)(2,1)S(1)}, bf16[256,128]{1,0:T(8,128)(2,1)S(1)}, bf16[256,128]{1,0:T(8,128)(2...) custom-call(bf16[1,1,1280,256]{3,2,1,0:T(8,128)(2,1)} %q_hbm.1, ...), custom_call_target="tpu_custom_call" | custom-call | flops 1677721600 | bytes 1966080 | tf_op jit(solution)/shard_map/pallas_call | solution.py:236
  15.1 2.4 %shard_map.38 = bf16[1,1,1280,256]{3,2,1,0:T(8,128)(2,1)} custom-call(bf16[1024,256]{1,0:T(8,128)(2,1)S(1)} %get-tuple-element.12.done_rows, bf16[512,128]{1,0:T(8,128)(2,1)S(1)} %get-tuple-element.13.query, bf16[256,128]{1,0:T(8,128)(2,1)S(1)} %get-tuple-element.14.key_tile, bf16[256,128]{1,0:T(8,128)(2,1)S(1)} %get-tuple-element.15.value_tile, ...), custom_call_target="tpu_custom_call" | custom-call | tf_op jit(solution)/shard_map/pallas_call | solution.py:266

commit v6 on v4

--- a/solution.py
+++ b/solution.py
@@ -71,6 +71,7 @@
 
     pieces = WINDOW // PIECE
     copies = [halo_copies(piece) for piece in range(pieces)]
+    copies[-2:] = [list(group) for group in zip(*copies[-2:])]
 
     @pl.when(jnp.logical_not(closing))
     def _():
@@ -95,12 +96,10 @@
 
     halo_bias = jnp.where(opening, LOWEST, 0.0).astype(jnp.float32)
 
-    def arrive(chunk):
-        per_chunk = TILE // PIECE
-        for piece in range((chunks - 1 - chunk) * per_chunk, (chunks - chunk) * per_chunk):
-
-            @pl.when(jnp.logical_not(opening))
-            def _():
+    def arrive(first, last):
+        @pl.when(jnp.logical_not(opening))
+        def _():
+            for piece in range(first, last):
                 for copy in copies[piece]:
                     copy.wait_recv()
 
@@ -172,14 +171,28 @@
         if block == 2:
             sent(next(refills))
     sent(next(refills))
-    for chunk in reversed(range(chunks)):
-        arrive(chunk)
+    per_chunk = TILE // PIECE
+    for chunk in reversed(range(1, chunks)):
+        arrive((chunks - 1 - chunk) * per_chunk, (chunks - chunk) * per_chunk)
         for block in reversed(range(chunk + 1)):
             states[block] = with_chunk(states[block], block, chunk)
             if block == chunk:
                 finish(chunk, states[chunk])
             if chunk == chunks - 1 and block == 2:
                 sent(next(refills))
+    top, row_total, gathered = states[0]
+    query = stacked_query(0)
+    arrive(pieces - 2, pieces - 1)
+    raw = scores_of(query, 0, 0)
+    new_top = jnp.maximum(top, jnp.max(raw, axis=1, keepdims=True) + halo_bias)
+    keep = jnp.exp2((top - new_top) * LOG2_SCALE)
+    probable = jnp.exp2(raw * LOG2_SCALE - (new_top * LOG2_SCALE - halo_bias))
+    weights = probable.astype(jnp.bfloat16)
+    row_total = row_total * keep + jnp.sum(probable, axis=1, keepdims=True)
+    gathered = gathered * keep
+    arrive(pieces - 1, pieces)
+    gathered = gathered + jnp.dot(weights, values[0:TILE, :], preferred_element_type=jnp.float32)
+    finish(0, (new_top, row_total, gathered))
     for piece in refills:
         sent(piece)
 

time: 16.6 us -> 16.4 us (0.988)
  Pallas kernels: 15.6 us -> 15.4 us
    pallas_call x1, Pallas kernels: 15.6 us -> 15.4 us  [per_device(): pl.pallas_call(functools.partial(attention_kernel, seq_count, mp_count),...]
where the time goes in v6:
time: 16.4 us; the launch traced here: 16.2 us
  Pallas kernels  15.4 us (94%)
  local copies, waits for them, and re-layouts  0.84 us (5%)
    pallas_call x1, Pallas kernels, per_device(): pl.pallas_call(functools.partial(attention_kernel, seq_count, mp_count),...  15.4 us
    unnamed x1, local copies, waits for them, and re-layouts  0.84 us

profile of v6, /device:TPU:4, one launch (start us, length us, event | category | flops | bytes accessed | tf_op | source)
XLA Modules:
  0.0 16.2 jit_solution(10427890326512572391)
XLA Ops:
  0.0 15.4 %shard_map.37 = bf16[1,1,1280,256]{3,2,1,0:T(8,128)(2,1)S(1)} custom-call(bf16[1,1,1280,256]{3,2,1,0:T(8,128)(2,1)} %q_hbm.1, bf16[1,1,1280,128]{3,2,1,0:T(8,128)(2,1)} %k_hbm.1, bf16[1,1,1280,128]{3,2,1,0:T(8,128)(2,1)} %v_hbm.1), custom_call_target="tpu_custom_call" | custom-call | flops 1677721600 | bytes 1966080 | tf_op jit(solution)/shard_map/pallas_call | solution.py:208
  15.4 0.8 %copy.5 = bf16[1,1,1280,256]{3,2,1,0:T(8,128)(2,1)} copy(bf16[1,1,1280,256]{3,2,1,0:T(8,128)(2,1)S(1)} %shard_map.37) | data formatting | bytes 1310720

commit v7 on v6

--- a/solution.py
+++ b/solution.py
@@ -13,7 +13,7 @@
 WINDOW = 1024
 TILE = 256
 PIECE = 128
-IN_FLIGHT = 5
+IN_FLIGHT = (6, 4)
 LOG2_SCALE = 168.0 ** (-0.5) * math.log2(math.e)
 LOWEST = -1e30
 
@@ -76,7 +76,13 @@
     @pl.when(jnp.logical_not(closing))
     def _():
         pl.semaphore_wait(barrier, 1)
-        for piece in range(min(IN_FLIGHT, pieces)):
+        for piece in range(min(IN_FLIGHT)):
+            for copy in copies[piece]:
+                copy.start()
+
+    @pl.when(jnp.logical_and(jnp.logical_not(closing), mp_index % 2 == 0))
+    def _():
+        for piece in range(min(IN_FLIGHT), IN_FLIGHT[0]):
             for copy in copies[piece]:
                 copy.start()
 
@@ -85,9 +91,14 @@
         def _():
             for copy in copies[piece]:
                 copy.wait_send()
-            if piece + IN_FLIGHT < pieces:
-                for copy in copies[piece + IN_FLIGHT]:
-                    copy.start()
+
+        for core, ahead in enumerate(IN_FLIGHT):
+            if piece + ahead < pieces:
+
+                @pl.when(jnp.logical_and(jnp.logical_not(closing), mp_index % 2 == core))
+                def _():
+                    for copy in copies[piece + ahead]:
+                        copy.start()
 
     @pl.when(opening)
     def _():
@@ -178,7 +189,7 @@
             states[block] = with_chunk(states[block], block, chunk)
             if block == chunk:
                 finish(chunk, states[chunk])
-            if chunk == chunks - 1 and block == 2:
+            if (chunk, block) in ((chunks - 1, 2), (chunks - 2, 1)):
                 sent(next(refills))
     top, row_total, gathered = states[0]
     query = stacked_query(0)

time: 16.4 us -> 16.4 us (level)
  no operation moved by 1% of the time
where the time goes in v7:
time: 16.4 us; the launch traced here: 16.2 us
  Pallas kernels  15.4 us (94%)
  local copies, waits for them, and re-layouts  0.84 us (5%)
    pallas_call x1, Pallas kernels, per_device(): pl.pallas_call(functools.partial(attention_kernel, seq_count, mp_count),...  15.4 us
    unnamed x1, local copies, waits for them, and re-layouts  0.84 us

profile of v7, /device:TPU:4, one launch (start us, length us, event | category | flops | bytes accessed | tf_op | source)
XLA Modules:
  0.0 16.2 jit_solution(9454873922841263474)
XLA Ops:
  0.0 15.4 %shard_map.37 = bf16[1,1,1280,256]{3,2,1,0:T(8,128)(2,1)S(1)} custom-call(bf16[1,1,1280,256]{3,2,1,0:T(8,128)(2,1)} %q_hbm.1, bf16[1,1,1280,128]{3,2,1,0:T(8,128)(2,1)} %k_hbm.1, bf16[1,1,1280,128]{3,2,1,0:T(8,128)(2,1)} %v_hbm.1), custom_call_target="tpu_custom_call" | custom-call | flops 1677721600 | bytes 1966080 | tf_op jit(solution)/shard_map/pallas_call | solution.py:219
  15.4 0.8 %copy.5 = bf16[1,1,1280,256]{3,2,1,0:T(8,128)(2,1)} copy(bf16[1,1,1280,256]{3,2,1,0:T(8,128)(2,1)S(1)} %shard_map.37) | data formatting | bytes 1310720
